TPU v7x, 32 devices: a whole 2x2x4 slice. The times are simulated.
32 devices in a mesh: roll: 4 (over x, core), tp: 8 (over z, y).
Axes of the slice: x: 2, y: 2, z: 4, core: 2. Of those that a mesh axis runs over, the one named last changes fastest.
Arguments:
- tokens: bfloat16 [128, 8, 2048], P(('roll', 'tp')), may hold values from -6 to 6
- lengths: int32 [128], P(('roll', 'tp')), may hold values from 1 to 8
- plan: int32 [2, 128, 1], P(None, ('roll', 'tp')), may hold values from 0 to 3, as said below
- owners: int32 [4], replicated, may hold values from 0 to 3, each once
- gate_up: float32 [4, 8, 2048, 768], P('roll', 'tp'), may hold values from -0.125 to 0.125
- down: float32 [4, 8, 384, 2048], P('roll', 'tp'), may hold values from -0.3125 to 0.3125
- norm_gain: float32 [2, 2048], replicated, may hold values from 0.5 to 1.5
- routing: int32 [2, 2048, 1], P(None, ('roll', 'tp')), may hold values from 0 to 7; in each aligned block of 64 rows (0 to 63, 64 to 127, ..., all dimensions but the last counted through in order) at most 10 rows name the same one
- route_weight: float32 [2, 2048], P(None, ('roll', 'tp')), may hold values from 0.1 to 1
Outputs:
- result: bfloat16 [128, 8, 2048], P(('roll', 'tp'))
Inputs may be any that keep to these rules, and one draw needn't show every extreme that they name: In layer 0 at most 2 rows of one device name the same owner, and every device's rows reach 2. For l >= 1, plan[l, i, 0] = (r + s_l[plan[l - 1, i, 0]]) mod 4, with r the roll index of row i's device and s_l a permutation of the owners drawn for layer l. owners is a permutation; layer l's master lies in the slot of roll index owners[l]. `routing`: every received token slot, empty ones included, names one window expert; of the 64 slots of one device at most 10 name the same expert, and in every draw some device reaches 10.
All inputs are finite; a program needn't handle non-finite values.
Results may differ from a plain program's by a relative error of at most 0.0048.
Values may be sent and summed in bfloat16 or wider, within the bound.
A program may use at most 128 MiB of HBM per device.

v0:
```python
import jax
import jax.numpy as jnp
from jax import lax
from jax.sharding import PartitionSpec as P

CAP = 2
epsilon = 1e-06


def spread(block, axis, owner):
    block = jnp.where(lax.axis_index(axis) == owner, block, jnp.zeros_like(block))
    return lax.psum(block, axis)


def slot_plan(target, groups, capacity):
    count = target.shape[0]
    earlier = jnp.arange(count)[None, :] < jnp.arange(count)[:, None]
    same = target[:, None] == target[None, :]
    within = jnp.sum(jnp.logical_and(same, earlier).astype(jnp.int32), axis=1)
    slot = target * capacity + within
    return (jnp.arange(groups * capacity)[:, None] == slot[None, :]).astype(jnp.bfloat16)


def into_slots(taken, items):
    flat = items.reshape(items.shape[0], -1)
    placed = jnp.dot(taken, flat, preferred_element_type=jnp.float32).astype(items.dtype)
    return placed.reshape((-1,) + items.shape[1:])


def from_slots(taken, slots):
    return into_slots(taken.T, slots)


def swap(value, distance):
    size = lax.axis_size("roll")
    return lax.ppermute(value, "roll", [(place, place ^ distance) for place in range(size)])


def share_halves(gate_up, down):
    upper = lax.rem(lax.axis_index("roll"), 2) == 1
    kept, given = ([], [])
    for master in (gate_up[0, 0], down[0, 0]):
        middle = master.shape[0] // 2
        low, high = (master[:middle].astype(jnp.bfloat16), master[middle:].astype(jnp.bfloat16))
        kept.append(jnp.where(upper, high, low))
        given.append(jnp.where(upper, low, high))
    return (kept, [swap(half, 1) for half in given])


def cross(kept, got, owner, before):
    me = lax.axis_index("roll")
    halves = [
        jnp.where(owner == me, mine, jnp.where(owner == me ^ 1, theirs, jnp.zeros_like(mine)))
        for mine, theirs in zip(kept, got)
    ]
    halves, _ = lax.optimization_barrier((halves, before))
    others = [jnp.zeros_like(half) for half in halves]
    distance = 2
    while distance < lax.axis_size("roll"):
        halves = [half + other for half, other in zip(halves, others)] if distance > 2 else halves
        others = [swap(half, distance) for half in halves]
        distance *= 2
    return (halves, others)


def complete(halves, others):
    upper = lax.rem(lax.axis_index("roll"), 2) == 1
    weights = []
    for half, other in zip(halves, others):
        half = half + other
        other = swap(half, 1)
        weights.append(
            jnp.concatenate([jnp.where(upper, other, half), jnp.where(upper, half, other)], axis=0)
        )
    return weights


def share_plan(plan, lengths, roll_size):
    layer_count, rows_dev = (plan.shape[0], plan.shape[1])
    packed = jnp.concatenate([plan[:, :, 0].reshape(-1), lengths])
    sent = jnp.broadcast_to(packed[None, :], (roll_size, packed.shape[0]))
    got = lax.all_to_all(sent, "roll", split_axis=0, concat_axis=0, tiled=True)
    return (got[:, :-rows_dev].reshape(roll_size, layer_count, rows_dev), got[:, -rows_dev:])


def held_lengths(owner, row_lengths):
    me, count = (lax.axis_index("roll"), owner.shape[1])
    earlier = jnp.arange(count)[None, :] < jnp.arange(count)[:, None]
    same = owner[:, :, None] == owner[:, None, :]
    within = jnp.sum(jnp.logical_and(same, earlier[None]).astype(jnp.int32), axis=2)
    here = jnp.logical_and(
        (owner == me)[:, None, :], within[:, None, :] == jnp.arange(CAP)[None, :, None]
    )
    return jnp.sum(jnp.where(here, row_lengths[:, None, :], 0), axis=2).reshape(-1)


def forward_plan(previous, owner, roll_size):
    me = lax.axis_index("roll")
    homes = jnp.arange(roll_size)
    turned = lax.rem(owner - homes[:, None] + roll_size, roll_size)
    turn = jnp.max(
        jnp.where(previous[:, :, None] == homes[None, None, :], turned[:, :, None], -1), axis=(0, 1)
    )
    mine = jnp.max(jnp.where(homes == me, turn, -1))
    to_send = jnp.logical_and(
        mine >= 0, homes[:, None] == lax.rem(homes[None, :] + mine, roll_size)
    )
    to_keep = jnp.logical_and(
        turn[None, :] >= 0, lax.rem(homes[:, None] + turn[None, :], roll_size) == me
    )
    return (to_send.astype(jnp.bfloat16), to_keep.astype(jnp.bfloat16))


def forward_rows(combined, moves, roll_size):
    chunks = into_slots(moves[0], combined.reshape((roll_size, CAP) + combined.shape[1:]))
    came = lax.all_to_all(chunks, "roll", split_axis=0, concat_axis=0, tiled=True)
    return into_slots(moves[1], came).reshape(combined.shape)


def send_home(combined, taken):
    home_rows = lax.all_to_all(combined, "roll", split_axis=0, concat_axis=0, tiled=True)
    return from_slots(taken, home_rows)


def process_rows(held, slot_lengths, crossing, first, layer_gain, route_column, weight_column):
    tp_size = lax.axis_size("tp")
    row_tokens = held.shape[1]
    model_width = held.shape[2]
    received = held.reshape(-1, model_width)
    token_count = received.shape[0]
    present = (jnp.arange(row_tokens)[None, :] < slot_lengths[:, None]).reshape(-1)
    widened = received.astype(jnp.float32)
    normed = (
        widened
        * lax.rsqrt(jnp.mean(widened * widened, axis=1, keepdims=True) + epsilon)
        * layer_gain[None, :]
    ).astype(jnp.bfloat16)
    expert_slots = 5 * token_count // (4 * tp_size)
    taken = slot_plan(route_column, tp_size, expert_slots)
    send_tokens = into_slots(taken, normed).reshape(tp_size, expert_slots, model_width)
    arrived = lax.all_to_all(send_tokens, "tp", split_axis=0, concat_axis=0, tiled=True)
    halves, others = crossing
    if first:
        others, arrived = lax.optimization_barrier((others, arrived))
    gate_up_w, down_w = complete(halves, others)
    hidden_width = down_w.shape[0]
    flattened = arrived.reshape(-1, model_width)
    projected = jnp.dot(flattened, gate_up_w, preferred_element_type=jnp.float32)
    hidden = (jax.nn.silu(projected[:, :hidden_width]) * projected[:, hidden_width:]).astype(
        jnp.bfloat16
    )
    produced = jnp.dot(hidden, down_w, preferred_element_type=jnp.float32).astype(jnp.bfloat16)
    returned = lax.all_to_all(
        produced.reshape(arrived.shape), "tp", split_axis=0, concat_axis=0, tiled=True
    )
    answer = from_slots(taken, returned.reshape(-1, model_width))
    combined = (
        widened
        + (present.astype(jnp.float32) * weight_column)[:, None] * answer.astype(jnp.float32)
    ).astype(jnp.bfloat16)
    return combined.reshape(held.shape)


def per_device(tokens, lengths, plan, owners, gate_up, down, norm_gain, routing, route_weight):
    layer_count = plan.shape[0]
    roll_size = lax.axis_size("roll")
    kept, got = share_halves(gate_up, down)
    home = slot_plan(plan[layer_count - 1, :, 0], roll_size, CAP)
    owner, row_lengths = share_plan(plan, lengths, roll_size)
    first_rows = into_slots(slot_plan(plan[0, :, 0], roll_size, CAP), tokens)
    held = lax.all_to_all(first_rows, "roll", split_axis=0, concat_axis=0, tiled=True)
    crossings, before = ([], (owner, row_lengths, held))
    for layer_index in range(layer_count):
        crossings.append(cross(kept, got, owners[layer_index], before))
        before = crossings[-1][1]
    for layer_index in range(layer_count):
        if layer_index > 0:
            moves = forward_plan(owner[:, layer_index - 1], owner[:, layer_index], roll_size)
            held = forward_rows(held, moves, roll_size)
        held = process_rows(
            held,
            held_lengths(owner[:, layer_index], row_lengths),
            crossings[layer_index],
            layer_index == 0,
            norm_gain[layer_index],
            routing[layer_index, :, 0],
            route_weight[layer_index],
        )
    current = send_home(held, home)
    return current


def solution(mesh):
    in_specs = (
        P(("roll", "tp"), None, None),
        P(("roll", "tp")),
        P(None, ("roll", "tp"), None),
        P(),
        P("roll", "tp", None, None),
        P("roll", "tp", None, None),
        P(),
        P(None, ("roll", "tp"), None),
        P(None, ("roll", "tp")),
    )
    out_specs = P(("roll", "tp"), None, None)
    return jax.shard_map(
        per_device, mesh=mesh, in_specs=in_specs, out_specs=out_specs, check_vma=False
    )
```

profile of v0, /device:TPU:0, one launch (start us, length us, event | category | flops | bytes accessed | tf_op | source)
XLA Modules:
  0.0 201.8 jit_solution(14525525016751189502)
XLA Ops:
  3.2 4.2 %all-to-all-start = ((s32[4,1,12]{2,1,0:T(1,128)}), s32[4,1,12]{2,1,0:T(1,128)S(1)}, u32[]{:S(2)}, u32[]{:S(2)}) async-start(s32[4,1,12]{2,1,0:T(1,128)} %broadcast_in_dim.29), calls=%async_computation | async-start | bytes 4096 | tf_op jit(solution)/shard_map/all_to_all | solution.py:82
  7.5 2.3 %convert.11 = bf16[1,1,384,2048]{3,2,1,0:T(8,128)(2,1)S(1)} convert(f32[1,1,384,2048]{3,2,1,0:T(8,128)} %param.14) | non-fusion elementwise | flops 786432 | bytes 4718592 | tf_op jit(solution)/shard_map/convert.3
  19.2 3.4 %all-to-all-start.1 = ((bf16[8,8,2048]{2,1,0:T(8,128)(2,1)}), bf16[8,8,2048]{2,1,0:T(8,128)(2,1)S(1)}, u32[]{:S(2)}, u32[]{:S(2)}) async-start(bf16[8,8,2048]{2,1,0:T(8,128)(2,1)} %copy.15), calls=%async_computation.1 | async-start | bytes 524288 | tf_op jit(solution)/shard_map/all_to_all | solution.py:171
  22.7 2.9 %bitcast_select_fusion.2 = (bf16[192,2048]{1,0:T(8,128)(2,1)}, bf16[192,2048]{1,0:T(8,128)(2,1)}) fusion(bf16[192,2048]{1,0:T(8,128)(2,1)} %collective-permute-done.1, pred[]{:T(512)S(6)} %eq.277, pred[]{:T(512)S(6)} %eq.276, bf16[1,1,384,2048]{3,2,1,0:T(8,128)(2,1)} %copy-done, pred[]{:T(512)S(6)} %eq.261, pred[]{:T(512)S(6)} %eq.262, pred[]{:T(512)S(6)} %eq.260), kind=kLoop, calls=%fused_computation.42 | loop fusion | flops 1966080 | bytes 3932165 | tf_op jit(solution)/shard_map/jit(_where)/select_n | solution.py:53
  25.7 3.3 %bitcast_select_fusion = (bf16[1024,768]{1,0:T(8,128)(2,1)}, bf16[1024,768]{1,0:T(8,128)(2,1)}) fusion(bf16[1024,768]{1,0:T(8,128)(2,1)} %collective-permute-done, pred[]{:T(512)S(6)} %eq.277, pred[]{:T(512)S(6)} %eq.276, bf16[1,1,2048,768]{3,2,1,0:T(8,128)(2,1)S(1)} %convert.10, pred[]{:T(512)S(6)} %eq.261, pred[]{:T(512)S(6)} %eq.262, pred[]{:T(512)S(6)} %eq.260), kind=kLoop, calls=%fused_computation.34 | loop fusion | flops 3932160 | bytes 7864325 | tf_op jit(solution)/shard_map/jit(_where)/select_n | solution.py:53
  29.0 2.0 collective-permute-start.2
  32.7 6.3 %all-to-all-start.2 = ((bf16[8,10,2048]{2,1,0:T(8,128)(2,1)}), bf16[8,10,2048]{2,1,0:T(8,128)(2,1)S(1)}, u32[]{:S(2)}, u32[]{:S(2)}) async-start(bf16[8,10,2048]{2,1,0:T(8,128)(2,1)} %reshape.238), calls=%async_computation.2 | async-start | bytes 1048576 | tf_op jit(solution)/shard_map/all_to_all | solution.py:141
  38.9 14.5 %all-to-all-done.2 = bf16[8,10,2048]{2,1,0:T(8,128)(2,1)S(1)} async-done(((bf16[8,10,2048]{2,1,0:T(8,128)(2,1)}), bf16[8,10,2048]{2,1,0:T(8,128)(2,1)S(1)}, u32[]{:S(2)}, u32[]{:S(2)}) %all-to-all-start.2) | async-done | bytes 327712 | tf_op jit(solution)/shard_map/all_to_all | solution.py:141
  53.5 29.4 %collective-permute-done.3 = bf16[192,2048]{1,0:T(8,128)(2,1)S(1)} collective-permute-done((bf16[192,2048]{1,0:T(8,128)(2,1)}, bf16[192,2048]{1,0:T(8,128)(2,1)S(1)}, u32[]{:S(2)}, u32[]{:S(2)}) %collective-permute-start.3) | collective-permute-done | bytes 786464 | tf_op jit(solution)/shard_map/ppermute | solution.py:36
  83.8 1.9 add.108
  88.2 1.9 reshape.239
  90.0 1.7 collective-permute-start.6
  93.2 1.7 broadcast_select_fusion.3
  96.9 6.3 %all-to-all-start.3 = ((bf16[8,10,2048]{2,1,0:T(8,128)(2,1)}), bf16[8,10,2048]{2,1,0:T(8,128)(2,1)}, u32[]{:S(2)}, u32[]{:S(2)}) async-start(bf16[8,10,2048]{2,1,0:T(8,128)(2,1)} %reshape.240), calls=%async_computation.3 | async-start | bytes 1048576 | tf_op jit(solution)/shard_map/all_to_all | solution.py:153
  106.1 21.3 %collective-permute-done.6 = bf16[1024,768]{1,0:T(8,128)(2,1)} collective-permute-done((bf16[1024,768]{1,0:T(8,128)(2,1)S(1)}, bf16[1024,768]{1,0:T(8,128)(2,1)}, u32[]{:S(2)}, u32[]{:S(2)}) %collective-permute-start.6) | collective-permute-done | bytes 1572896 | tf_op jit(solution)/shard_map/ppermute | solution.py:36
  127.4 1.8 add.114
  132.1 3.4 %all-to-all-start.4 = ((bf16[4,2,8,2048]{3,2,1,0:T(8,128)(2,1)}), bf16[4,2,8,2048]{3,2,1,0:T(8,128)(2,1)S(1)}, u32[]{:S(2)}, u32[]{:S(2)}) async-start(bf16[4,2,8,2048]{3,2,1,0:T(8,128)(2,1)} %bitcast.78), calls=%async_computation.4 | async-start | bytes 524288 | tf_op jit(solution)/shard_map/all_to_all | solution.py:116
  135.5 8.8 %collective-permute-done.8 = bf16[192,2048]{1,0:T(8,128)(2,1)} collective-permute-done((bf16[192,2048]{1,0:T(8,128)(2,1)}, bf16[192,2048]{1,0:T(8,128)(2,1)}, u32[]{:S(2)}, u32[]{:S(2)}) %collective-permute-start.8) | collective-permute-done | bytes 786464 | tf_op jit(solution)/shard_map/ppermute | solution.py:36
  144.3 1.6 add.116
  148.3 6.3 %all-to-all-start.5 = ((bf16[8,10,2048]{2,1,0:T(8,128)(2,1)}), bf16[8,10,2048]{2,1,0:T(8,128)(2,1)S(1)}, u32[]{:S(2)}, u32[]{:S(2)}) async-start(bf16[8,10,2048]{2,1,0:T(8,128)(2,1)} %reshape.244), calls=%async_computation.5 | async-start | bytes 1048576 | tf_op jit(solution)/shard_map/all_to_all | solution.py:141
  154.6 2.4 %broadcast_select_fusion.6 = (bf16[192,2048]{1,0:T(8,128)(2,1)}, bf16[192,2048]{1,0:T(8,128)(2,1)}) fusion(bf16[192,2048]{1,0:T(8,128)(2,1)} %collective-permute-done.9, bf16[192,2048]{1,0:T(8,128)(2,1)S(1)} %add.116, pred[]{:T(512)S(6)} %eq.261), kind=kLoop, calls=%fused_computation.46 | loop fusion | flops 786432 | bytes 3145729 | tf_op jit(solution)/shard_map/jit(_where)/select_n | solution.py:73
  157.0 12.7 %all-to-all-done.5 = bf16[8,10,2048]{2,1,0:T(8,128)(2,1)S(1)} async-done(((bf16[8,10,2048]{2,1,0:T(8,128)(2,1)}), bf16[8,10,2048]{2,1,0:T(8,128)(2,1)S(1)}, u32[]{:S(2)}, u32[]{:S(2)}) %all-to-all-start.5) | async-done | bytes 327712 | tf_op jit(solution)/shard_map/all_to_all | solution.py:141
  173.4 18.1 %all_to_all.44 = bf16[8,10,2048]{2,1,0:T(8,128)(2,1)S(1)} all-to-all(bf16[8,10,2048]{2,1,0:T(8,128)(2,1)S(1)} %reshape.246), channel_id=1, replica_groups=mesh['roll'=4,'tp'=8] {'tp'}, dimensions={0} | all-to-all | bytes 655360 | tf_op jit(solution)/shard_map/all_to_all | solution.py:153
  191.9 8.8 %all_to_all.45 = bf16[8,8,2048]{2,1,0:T(8,128)(2,1)S(1)} all-to-all(bf16[8,8,2048]{2,1,0:T(8,128)(2,1)S(1)} %fusion.17), channel_id=1, replica_groups=mesh['roll'=4,'tp'=8] {'roll'}, dimensions={0} | all-to-all | bytes 524288 | tf_op jit(solution)/shard_map/all_to_all | solution.py:121
  (127 shorter events, 31.3 us)
Async XLA Ops:
  3.2 15.9 %all-to-all-start = ((s32[4,1,12]{2,1,0:T(1,128)}), s32[4,1,12]{2,1,0:T(1,128)S(1)}, u32[]{:S(2)}, u32[]{:S(2)}) async-start(s32[4,1,12]{2,1,0:T(1,128)} %broadcast_in_dim.29), calls=%async_computation | async-start | bytes 4096 | tf_op jit(solution)/shard_map/all_to_all | solution.py:82
  7.5 4.6 %copy-start.1 = (f32[1,1,2048,768]{3,2,1,0:T(8,128)S(1)}, f32[1,1,2048,768]{3,2,1,0:T(8,128)}, u32[]{:S(2)}) copy-start(f32[1,1,2048,768]{3,2,1,0:T(8,128)} %param.13) | copy-start | bytes 18874372
  11.2 11.6 %collective-permute-start.1 = (bf16[192,2048]{1,0:T(8,128)(2,1)}, bf16[192,2048]{1,0:T(8,128)(2,1)}, u32[]{:S(2)}, u32[]{:S(2)}) collective-permute-start(bf16[192,2048]{1,0:T(8,128)(2,1)} %select_bitcast_fusion.1), channel_id=1, source_target_pairs={{0,8},{8,0},{16,24},{24,16},{1,9},{9,1},{17,25},{25,17},{2,10},{10... | collective-permute-start | bytes 2359304 | tf_op jit(solution)/shard_map/ppermute | solution.py:36
  12.4 5.3 %copy-start.11 = (bf16[4,8,2048]{2,1,0:T(8,128)(2,1)S(1)}, bf16[4,8,2048]{2,1,0:T(8,128)(2,1)}, u32[]{:S(2)}) copy-start(bf16[4,8,2048]{2,1,0:T(8,128)(2,1)} %param.9) | copy-start | bytes 393220
  12.4 5.4 %copy-start.13 = (s32[2,4,1]{1,2,0:T(1,128)S(1)}, s32[2,4,1]{1,2,0:T(1,128)}, u32[]{:S(2)}) copy-start(s32[2,4,1]{1,2,0:T(1,128)} %param.11) | copy-start | bytes 100
  13.7 11.9 %collective-permute-start = (bf16[1024,768]{1,0:T(8,128)(2,1)}, bf16[1024,768]{1,0:T(8,128)(2,1)}, u32[]{:S(2)}, u32[]{:S(2)}) collective-permute-start(bf16[1024,768]{1,0:T(8,128)(2,1)} %select_bitcast_fusion), channel_id=1, source_target_pairs={{0,8},{8,0},{16,24},{24,16},{1,9},{9,1},{17,25},{25,17},{2,10},{10... | collective-permute-start | bytes 4718600 | tf_op jit(solution)/shard_map/ppermute | solution.py:36
  19.2 9.9 %all-to-all-start.1 = ((bf16[8,8,2048]{2,1,0:T(8,128)(2,1)}), bf16[8,8,2048]{2,1,0:T(8,128)(2,1)S(1)}, u32[]{:S(2)}, u32[]{:S(2)}) async-start(bf16[8,8,2048]{2,1,0:T(8,128)(2,1)} %copy.15), calls=%async_computation.1 | async-start | bytes 524288 | tf_op jit(solution)/shard_map/all_to_all | solution.py:171
  25.7 5.3 %copy-start.12 = (f32[2,2048]{1,0:T(2,128)S(1)}, f32[2,2048]{1,0:T(2,128)}, u32[]{:S(2)}) copy-start(f32[2,2048]{1,0:T(2,128)} %param.15) | copy-start | bytes 49156
  29.0 54.8 %copy-start.3 = (bf16[1024,768]{1,0:T(8,128)(2,1)S(1)}, bf16[1024,768]{1,0:T(8,128)(2,1)}, u32[]{:S(2)}) copy-start(bf16[1024,768]{1,0:T(8,128)(2,1)} %get-tuple-element.12) | copy-start | bytes 4718596
  29.0 54.8 %collective-permute-start.2 = (bf16[1024,768]{1,0:T(8,128)(2,1)}, bf16[1024,768]{1,0:T(8,128)(2,1)}, u32[]{:S(2)}, u32[]{:S(2)}) collective-permute-start(bf16[1024,768]{1,0:T(8,128)(2,1)} %get-tuple-element.12), channel_id=1, source_target_pairs={{0,16},{8,24},{16,0},{24,8},{1,17},{9,25},{17,1},{25,9},{2,18},{10... | collective-permute-start | bytes 4718600 | tf_op jit(solution)/shard_map/ppermute | solution.py:36
  31.4 51.5 %collective-permute-start.3 = (bf16[192,2048]{1,0:T(8,128)(2,1)}, bf16[192,2048]{1,0:T(8,128)(2,1)S(1)}, u32[]{:S(2)}, u32[]{:S(2)}) collective-permute-start(bf16[192,2048]{1,0:T(8,128)(2,1)} %get-tuple-element.13), channel_id=1, source_target_pairs={{0,16},{8,24},{16,0},{24,8},{1,17},{9,25},{17,1},{25,9},{2,18},{10... | collective-permute-start | bytes 2359304 | tf_op jit(solution)/shard_map/ppermute | solution.py:36
  32.7 20.8 %all-to-all-start.2 = ((bf16[8,10,2048]{2,1,0:T(8,128)(2,1)}), bf16[8,10,2048]{2,1,0:T(8,128)(2,1)S(1)}, u32[]{:S(2)}, u32[]{:S(2)}) async-start(bf16[8,10,2048]{2,1,0:T(8,128)(2,1)} %reshape.238), calls=%async_computation.2 | async-start | bytes 1048576 | tf_op jit(solution)/shard_map/all_to_all | solution.py:141
  53.5 29.4 %copy-start.5 = (bf16[8,10,2048]{2,1,0:T(8,128)(2,1)}, bf16[8,10,2048]{2,1,0:T(8,128)(2,1)S(1)}, u32[]{:S(2)}) copy-start(bf16[8,10,2048]{2,1,0:T(8,128)(2,1)S(1)} %all-to-all-done.2) | copy-start | bytes 983044
  53.5 32.2 %copy-start.4 = (bf16[192,2048]{1,0:T(8,128)(2,1)S(1)}, bf16[192,2048]{1,0:T(8,128)(2,1)}, u32[]{:S(2)}) copy-start(bf16[192,2048]{1,0:T(8,128)(2,1)} %get-tuple-element.13) | copy-start | bytes 2359300
  85.6 7.6 %collective-permute-start.4 = (bf16[1024,768]{1,0:T(8,128)(2,1)S(1)}, bf16[1024,768]{1,0:T(8,128)(2,1)}, u32[]{:S(2)}, u32[]{:S(2)}) collective-permute-start(bf16[1024,768]{1,0:T(8,128)(2,1)S(1)} %add.108), channel_id=1, source_target_pairs={{0,8},{8,0},{16,24},{24,16},{1,9},{9,1},{17,25},{25,17},{2,10},{10... | collective-permute-start | bytes 4718600 | tf_op jit(solution)/shard_map/ppermute | solution.py:36
  86.9 4.8 %collective-permute-start.5 = (bf16[192,2048]{1,0:T(8,128)(2,1)}, bf16[192,2048]{1,0:T(8,128)(2,1)}, u32[]{:S(2)}, u32[]{:S(2)}) collective-permute-start(bf16[192,2048]{1,0:T(8,128)(2,1)} %add.110), channel_id=1, source_target_pairs={{0,8},{8,0},{16,24},{24,16},{1,9},{9,1},{17,25},{25,17},{2,10},{10... | collective-permute-start | bytes 2359304 | tf_op jit(solution)/shard_map/ppermute | solution.py:36
  90.0 37.4 %collective-permute-start.6 = (bf16[1024,768]{1,0:T(8,128)(2,1)S(1)}, bf16[1024,768]{1,0:T(8,128)(2,1)}, u32[]{:S(2)}, u32[]{:S(2)}) collective-permute-start(bf16[1024,768]{1,0:T(8,128)(2,1)S(1)} %copy-done.2), channel_id=1, source_target_pairs={{0,16},{8,24},{16,0},{24,8},{1,17},{9,25},{17,1},{25,9},{2,18},{10... | collective-permute-start | bytes 4718600 | tf_op jit(solution)/shard_map/ppermute | solution.py:36
  96.0 8.9 %copy-start.16 = (f32[2,64]{1,0:T(2,128)S(1)}, f32[2,64]{1,0:T(2,128)}, u32[]{:S(2)}) copy-start(f32[2,64]{1,0:T(2,128)} %param.17) | copy-start | bytes 1540
  96.9 32.4 %all-to-all-start.3 = ((bf16[8,10,2048]{2,1,0:T(8,128)(2,1)}), bf16[8,10,2048]{2,1,0:T(8,128)(2,1)}, u32[]{:S(2)}, u32[]{:S(2)}) async-start(bf16[8,10,2048]{2,1,0:T(8,128)(2,1)} %reshape.240), calls=%async_computation.3 | async-start | bytes 1048576 | tf_op jit(solution)/shard_map/all_to_all | solution.py:153
  104.9 39.4 %collective-permute-start.8 = (bf16[192,2048]{1,0:T(8,128)(2,1)}, bf16[192,2048]{1,0:T(8,128)(2,1)}, u32[]{:S(2)}, u32[]{:S(2)}) collective-permute-start(bf16[192,2048]{1,0:T(8,128)(2,1)} %get-tuple-element.18), channel_id=1, source_target_pairs={{0,16},{8,24},{16,0},{24,8},{1,17},{9,25},{17,1},{25,9},{2,18},{10... | collective-permute-start | bytes 2359304 | tf_op jit(solution)/shard_map/ppermute | solution.py:36
  129.2 40.6 %collective-permute-start.7 = (bf16[1024,768]{1,0:T(8,128)(2,1)S(1)}, bf16[1024,768]{1,0:T(8,128)(2,1)}, u32[]{:S(2)}, u32[]{:S(2)}) collective-permute-start(bf16[1024,768]{1,0:T(8,128)(2,1)S(1)} %add.114), channel_id=1, source_target_pairs={{0,8},{8,0},{16,24},{24,16},{1,9},{9,1},{17,25},{25,17},{2,10},{10... | collective-permute-start | bytes 4718600 | tf_op jit(solution)/shard_map/ppermute | solution.py:36
  132.1 14.0 %all-to-all-start.4 = ((bf16[4,2,8,2048]{3,2,1,0:T(8,128)(2,1)}), bf16[4,2,8,2048]{3,2,1,0:T(8,128)(2,1)S(1)}, u32[]{:S(2)}, u32[]{:S(2)}) async-start(bf16[4,2,8,2048]{3,2,1,0:T(8,128)(2,1)} %bitcast.78), calls=%async_computation.4 | async-start | bytes 524288 | tf_op jit(solution)/shard_map/all_to_all | solution.py:116
  145.9 8.7 %collective-permute-start.9 = (bf16[192,2048]{1,0:T(8,128)(2,1)S(1)}, bf16[192,2048]{1,0:T(8,128)(2,1)}, u32[]{:S(2)}, u32[]{:S(2)}) collective-permute-start(bf16[192,2048]{1,0:T(8,128)(2,1)S(1)} %add.116), channel_id=1, source_target_pairs={{0,8},{8,0},{16,24},{24,16},{1,9},{9,1},{17,25},{25,17},{2,10},{10... | collective-permute-start | bytes 2359304 | tf_op jit(solution)/shard_map/ppermute | solution.py:36
  148.3 21.4 %all-to-all-start.5 = ((bf16[8,10,2048]{2,1,0:T(8,128)(2,1)}), bf16[8,10,2048]{2,1,0:T(8,128)(2,1)S(1)}, u32[]{:S(2)}, u32[]{:S(2)}) async-start(bf16[8,10,2048]{2,1,0:T(8,128)(2,1)} %reshape.244), calls=%async_computation.5 | async-start | bytes 1048576 | tf_op jit(solution)/shard_map/all_to_all | solution.py:141
  (9 other events, 16.7 us)
where the time goes:
time: 203 us; the launch traced here: 202 us
  waiting for transfers between devices  86.7 us (43%)
  starting transfers between devices  35.8 us (18%)
  other arithmetic  29.4 us (14%)
  blocking collectives  26.9 us (13%)
  local copies, waits for them, and re-layouts  14.8 us (7%)
  matrix products  4.39 us (2%)
  between operations  3.76 us (2%)
    ppermute x10, waiting for transfers between devices, swap(): lax.ppermute(value, 'roll', [(place, place ^ distance) for place in range...  59.4 us
    all_to_all x2, waiting for transfers between devices, process_rows(): lax.all_to_all(send_tokens, 'tp', split_axis=0, concat_axis=0, tiled=True)  27.2 us
    all_to_all x1, blocking collectives, process_rows(): lax.all_to_all(produced.reshape(arrived.shape), 'tp', split_axis=0, conca...  18.1 us
    all_to_all x2, starting transfers between devices, process_rows(): lax.all_to_all(send_tokens, 'tp', split_axis=0, concat_axis=0, tiled=True)  12.5 us
    all_to_all x1, blocking collectives, send_home(): lax.all_to_all(combined, 'roll', split_axis=0, concat_axis=0, tiled=True)  8.77 us
    select_n x4, other arithmetic, complete(): jnp.where(upper, other, half)  7.14 us
    add x4, other arithmetic, complete(): half = half + other  6.47 us
    select_n x2, other arithmetic, cross(): jnp.where(owner == me, mine, jnp.where(owner == me ^ 1, theirs, jnp.zeros...  6.27 us
  transfers between devices with their start and end apart: 16, of which 6 were waited for; matrix products, arithmetic and copies ran while one was open for 18% of the time, Pallas kernels for 0%

commit v1 on v0

--- a/solution.py
+++ b/solution.py
@@ -5,6 +5,29 @@
 
 CAP = 2
 epsilon = 1e-06
+
+
+def in_blocks(x, dim, size):
+    shape = x.shape
+    blocks = x.reshape(*shape[:dim], size, shape[dim] // size, *shape[dim + 1 :])
+    return jnp.moveaxis(blocks, dim, 0)
+
+
+def laid_out(blocks, dim):
+    shape = list(blocks.shape[1:])
+    shape[dim] *= blocks.shape[0]
+    return jnp.moveaxis(blocks, 0, dim).reshape(shape)
+
+
+def exchange_directly(array, axis, split_dim, concat_dim):
+    size, place = (lax.axis_size(axis), lax.axis_index(axis))
+    tiles = in_blocks(array, split_dim, size)
+    gathered = [tiles[place]]
+    for step in range(1, size):
+        sent = tiles[(place + step) % size]
+        gathered.append(lax.ppermute(sent, axis, [(i, (i + step) % size) for i in range(size)]))
+    tiles = jnp.stack(gathered)[(place - jnp.arange(size)) % size]
+    return laid_out(tiles, concat_dim)
 
 
 def spread(block, axis, owner):
@@ -150,9 +173,7 @@
         jnp.bfloat16
     )
     produced = jnp.dot(hidden, down_w, preferred_element_type=jnp.float32).astype(jnp.bfloat16)
-    returned = lax.all_to_all(
-        produced.reshape(arrived.shape), "tp", split_axis=0, concat_axis=0, tiled=True
-    )
+    returned = exchange_directly(produced.reshape(arrived.shape), "tp", 0, 0)
     answer = from_slots(taken, returned.reshape(-1, model_width))
     combined = (
         widened

time: 203 us -> 227 us (1.12)
  waiting for transfers between devices: 86.7 us -> 109 us
  blocking collectives: 26.9 us -> 8.42 us
  starting transfers between devices: 35.8 us -> 48.5 us
  local copies, waits for them, and re-layouts: 14.8 us -> 19.8 us
    ppermute x0 -> x14, waiting for transfers between devices: none -> 27.5 us  [exchange_directly(): lax.ppermute(sent, axis, [(i, (i + step) % size) for i in range(size)])]
    ppermute x0 -> x14, starting transfers between devices: none -> 20.8 us  [exchange_directly(): lax.ppermute(sent, axis, [(i, (i + step) % size) for i in range(size)])]
    all_to_all x1 -> x0, blocking collectives: 18.1 us -> none  [process_rows(): lax.all_to_all(produced.reshape(arrived.shape), 'tp', split_axis=0, conca...]
    ppermute x10, waiting for transfers between devices: 59.4 us -> 50.7 us  [swap(): lax.ppermute(value, 'roll', [(place, place ^ distance) for place in range...]
    all_to_all x1 -> x0, starting transfers between devices: 6.27 us -> none  [process_rows(): lax.all_to_all(produced.reshape(arrived.shape), 'tp', split_axis=0, conca...]
    all_to_all x1, waiting for transfers between devices: 0.06 us -> 3.77 us  [forward_rows(): lax.all_to_all(chunks, 'roll', split_axis=0, concat_axis=0, tiled=True)]
    reshape x4 -> x0, local copies, waits for them, and re-layouts: 2.28 us -> none  [the longest x2 1.28 us: process_rows(): answer = from_slots(taken, returned.reshape(-1, model_width))]
    unnamed x42 -> x78, local copies, waits for them, and re-layouts: 5.13 us -> 6.82 us
  transfers between devices with their start and end apart: 16 -> 29, of which waited for: 6 -> 10; matrix products, arithmetic and copies ran while one was open for 18% -> 19% of each run, Pallas kernels for 0% -> 0%
where the time goes in v1:
time: 227 us; the launch traced here: 226 us
  waiting for transfers between devices  109 us (48%)
  starting transfers between devices  48.5 us (21%)
  other arithmetic  31.3 us (14%)
  local copies, waits for them, and re-layouts  19.8 us (9%)
  blocking collectives  8.42 us (4%)
  matrix products  5.2 us (2%)
  between operations  3.81 us (2%)
    ppermute x10, waiting for transfers between devices, swap(): lax.ppermute(value, 'roll', [(place, place ^ distance) for place in range...  50.7 us
    ppermute x14, waiting for transfers between devices, exchange_directly(): lax.ppermute(sent, axis, [(i, (i + step) % size) for i in range(size)])  27.5 us
    all_to_all x2, waiting for transfers between devices, process_rows(): lax.all_to_all(send_tokens, 'tp', split_axis=0, concat_axis=0, tiled=True)  26.8 us
    ppermute x14, starting transfers between devices, exchange_directly(): lax.ppermute(sent, axis, [(i, (i + step) % size) for i in range(size)])  20.8 us
    all_to_all x2, starting transfers between devices, process_rows(): lax.all_to_all(send_tokens, 'tp', split_axis=0, concat_axis=0, tiled=True)  10.4 us
    all_to_all x1, blocking collectives, send_home(): lax.all_to_all(combined, 'roll', split_axis=0, concat_axis=0, tiled=True)  8.42 us
    select_n x4, other arithmetic, complete(): jnp.where(upper, other, half)  7.13 us
    unnamed x78, local copies, waits for them, and re-layouts  6.82 us
  transfers between devices with their start and end apart: 29, of which 10 were waited for; matrix products, arithmetic and copies ran while one was open for 19% of the time, Pallas kernels for 0%

profile of v1, /device:TPU:0, one launch (start us, length us, event | category | flops | bytes accessed | tf_op | source)
XLA Modules:
  0.0 225.7 jit_solution(16328000387018531007)
XLA Ops:
  3.2 4.2 %all-to-all-start = ((s32[4,1,12]{2,1,0:T(1,128)}), s32[4,1,12]{2,1,0:T(1,128)S(1)}, u32[]{:S(2)}, u32[]{:S(2)}) async-start(s32[4,1,12]{2,1,0:T(1,128)} %broadcast_in_dim.29), calls=%async_computation | async-start | bytes 4096 | tf_op jit(solution)/shard_map/all_to_all | solution.py:105
  7.5 2.3 convert.11
  19.9 3.4 %all-to-all-start.1 = ((bf16[8,8,2048]{2,1,0:T(8,128)(2,1)}), bf16[8,8,2048]{2,1,0:T(8,128)(2,1)S(1)}, u32[]{:S(2)}, u32[]{:S(2)}) async-start(bf16[8,8,2048]{2,1,0:T(8,128)(2,1)} %copy.15), calls=%async_computation.1 | async-start | bytes 524288 | tf_op jit(solution)/shard_map/all_to_all | solution.py:192
  23.3 2.9 %bitcast_select_fusion.2 = (bf16[192,2048]{1,0:T(8,128)(2,1)}, bf16[192,2048]{1,0:T(8,128)(2,1)}) fusion(bf16[192,2048]{1,0:T(8,128)(2,1)} %collective-permute-done.1, pred[]{:T(512)S(6)} %eq.295, pred[]{:T(512)S(6)} %eq.294, bf16[1,1,384,2048]{3,2,1,0:T(8,128)(2,1)} %copy-done, pred[]{:T(512)S(6)} %eq.279, pred[]{:T(512)S(6)} %eq.280, pred[]{:T(512)S(6)} %eq.278), kind=kLoop, calls=%fused_computation.44 | loop fusion | flops 1966080 | bytes 3932165 | tf_op jit(solution)/shard_map/jit(_where)/select_n | solution.py:76
  26.3 3.4 %bitcast_select_fusion = (bf16[1024,768]{1,0:T(8,128)(2,1)}, bf16[1024,768]{1,0:T(8,128)(2,1)}) fusion(bf16[1024,768]{1,0:T(8,128)(2,1)} %collective-permute-done, pred[]{:T(512)S(6)} %eq.295, pred[]{:T(512)S(6)} %eq.294, bf16[1,1,2048,768]{3,2,1,0:T(8,128)(2,1)S(1)} %convert.10, pred[]{:T(512)S(6)} %eq.279, pred[]{:T(512)S(6)} %eq.280, pred[]{:T(512)S(6)} %eq.278), kind=kLoop, calls=%fused_computation.36 | loop fusion | flops 3932160 | bytes 7864325 | tf_op jit(solution)/shard_map/jit(_where)/select_n | solution.py:76
  33.3 6.3 %all-to-all-start.2 = ((bf16[8,10,2048]{2,1,0:T(8,128)(2,1)}), bf16[8,10,2048]{2,1,0:T(8,128)(2,1)}, u32[]{:S(2)}, u32[]{:S(2)}) async-start(bf16[8,10,2048]{2,1,0:T(8,128)(2,1)} %reshape.275), calls=%async_computation.2 | async-start | bytes 1048576 | tf_op jit(solution)/shard_map/all_to_all | solution.py:164
  39.6 14.6 %all-to-all-done.2 = bf16[8,10,2048]{2,1,0:T(8,128)(2,1)} async-done(((bf16[8,10,2048]{2,1,0:T(8,128)(2,1)}), bf16[8,10,2048]{2,1,0:T(8,128)(2,1)}, u32[]{:S(2)}, u32[]{:S(2)}) %all-to-all-start.2) | async-done | bytes 327712 | tf_op jit(solution)/shard_map/all_to_all | solution.py:164
  54.2 29.2 %collective-permute-done.3 = bf16[192,2048]{1,0:T(8,128)(2,1)S(1)} collective-permute-done((bf16[192,2048]{1,0:T(8,128)(2,1)}, bf16[192,2048]{1,0:T(8,128)(2,1)S(1)}, u32[]{:S(2)}, u32[]{:S(2)}) %collective-permute-start.3) | collective-permute-done | bytes 786464 | tf_op jit(solution)/shard_map/ppermute | solution.py:59
  103.1 3.0 %collective-permute-start.12 = (bf16[1,10,2048]{2,1,0:T(8,128)(2,1)S(1)}, bf16[1,10,2048]{2,1,0:T(8,128)(2,1)S(1)}, u32[]{:S(2)}, u32[]{:S(2)}) collective-permute-start(bf16[1,10,2048]{2,1,0:T(8,128)(2,1)S(1)} %get-tuple-element.44), channel_id=1, source_target_pairs={{0,7},{1,0},{2,1},{3,2},{4,3},{5,4},{6,5},{7,6},{8,15},{9,8},{10,9... | collective-permute-start | bytes 122888 | tf_op jit(solution)/shard_map/ppermute | solution.py:28
  108.1 21.5 %collective-permute-done.13 = bf16[1024,768]{1,0:T(8,128)(2,1)} collective-permute-done((bf16[1024,768]{1,0:T(8,128)(2,1)S(1)}, bf16[1024,768]{1,0:T(8,128)(2,1)}, u32[]{:S(2)}, u32[]{:S(2)}) %collective-permute-start.13) | collective-permute-done | bytes 1572896 | tf_op jit(solution)/shard_map/ppermute | solution.py:59
  129.6 4.0 %collective-permute-start.10 = (bf16[1,10,2048]{2,1,0:T(8,128)(2,1)}, bf16[1,10,2048]{2,1,0:T(8,128)(2,1)S(1)}, u32[]{:S(2)}, u32[]{:S(2)}) collective-permute-start(bf16[1,10,2048]{2,1,0:T(8,128)(2,1)} %get-tuple-element.46), channel_id=1, source_target_pairs={{0,5},{1,6},{2,7},{3,0},{4,1},{5,2},{6,3},{7,4},{8,13},{9,14},{10,... | collective-permute-start | bytes 122888 | tf_op jit(solution)/shard_map/ppermute | solution.py:28
  138.0 3.6 %collective-permute-done.7 = bf16[1,10,2048]{2,1,0:T(8,128)(2,1)S(1)} collective-permute-done((bf16[1,10,2048]{2,1,0:T(8,128)(2,1)S(1)}, bf16[1,10,2048]{2,1,0:T(8,128)(2,1)S(1)}, u32[]{:S(2)}, u32[]{:S(2)}) %collective-permute-start.7) | collective-permute-done | bytes 40992 | tf_op jit(solution)/shard_map/ppermute | solution.py:28
  141.6 6.2 %collective-permute-done.8 = bf16[1,10,2048]{2,1,0:T(8,128)(2,1)S(1)} collective-permute-done((bf16[1,10,2048]{2,1,0:T(8,128)(2,1)S(1)}, bf16[1,10,2048]{2,1,0:T(8,128)(2,1)S(1)}, u32[]{:S(2)}, u32[]{:S(2)}) %collective-permute-start.8) | collective-permute-done | bytes 40992 | tf_op jit(solution)/shard_map/ppermute | solution.py:28
  147.8 5.2 %collective-permute-done.9 = bf16[1,10,2048]{2,1,0:T(8,128)(2,1)S(1)} collective-permute-done((bf16[1,10,2048]{2,1,0:T(8,128)(2,1)S(1)}, bf16[1,10,2048]{2,1,0:T(8,128)(2,1)S(1)}, u32[]{:S(2)}, u32[]{:S(2)}) %collective-permute-start.9) | collective-permute-done | bytes 40992 | tf_op jit(solution)/shard_map/ppermute | solution.py:28
  157.3 3.4 %all-to-all-start.3 = ((bf16[4,2,8,2048]{3,2,1,0:T(8,128)(2,1)}), bf16[4,2,8,2048]{3,2,1,0:T(8,128)(2,1)S(1)}, u32[]{:S(2)}, u32[]{:S(2)}) async-start(bf16[4,2,8,2048]{3,2,1,0:T(8,128)(2,1)} %bitcast.138), calls=%async_computation.3 | async-start | bytes 524288 | tf_op jit(solution)/shard_map/all_to_all | solution.py:139
  163.0 3.8 %all-to-all-done.3 = bf16[4,2,8,2048]{3,2,1,0:T(8,128)(2,1)S(1)} async-done(((bf16[4,2,8,2048]{3,2,1,0:T(8,128)(2,1)}), bf16[4,2,8,2048]{3,2,1,0:T(8,128)(2,1)S(1)}, u32[]{:S(2)}, u32[]{:S(2)}) %all-to-all-start.3) | async-done | bytes 262176 | tf_op jit(solution)/shard_map/all_to_all | solution.py:139
  170.9 4.1 %all-to-all-start.4 = ((bf16[8,10,2048]{2,1,0:T(8,128)(2,1)}), bf16[8,10,2048]{2,1,0:T(8,128)(2,1)}, u32[]{:S(2)}, u32[]{:S(2)}) async-start(bf16[8,10,2048]{2,1,0:T(8,128)(2,1)} %reshape.279), calls=%async_computation.4 | async-start | bytes 1048576 | tf_op jit(solution)/shard_map/all_to_all | solution.py:164
  175.0 2.4 %broadcast_select_fusion.6 = (bf16[192,2048]{1,0:T(8,128)(2,1)}, bf16[192,2048]{1,0:T(8,128)(2,1)}) fusion(bf16[192,2048]{1,0:T(8,128)(2,1)} %collective-permute-done.16, bf16[192,2048]{1,0:T(8,128)(2,1)S(1)} %add.255, pred[]{:T(512)S(6)} %eq.279), kind=kLoop, calls=%fused_computation.48 | loop fusion | flops 786432 | bytes 3145729 | tf_op jit(solution)/shard_map/jit(_where)/select_n | solution.py:96
  177.4 12.2 %all-to-all-done.4 = bf16[8,10,2048]{2,1,0:T(8,128)(2,1)} async-done(((bf16[8,10,2048]{2,1,0:T(8,128)(2,1)}), bf16[8,10,2048]{2,1,0:T(8,128)(2,1)}, u32[]{:S(2)}, u32[]{:S(2)}) %all-to-all-start.4) | async-done | bytes 327712 | tf_op jit(solution)/shard_map/all_to_all | solution.py:164
  195.9 3.3 %collective-permute-start.23 = (bf16[1,10,2048]{2,1,0:T(8,128)(2,1)S(1)}, bf16[1,10,2048]{2,1,0:T(8,128)(2,1)S(1)}, u32[]{:S(2)}, u32[]{:S(2)}) collective-permute-start(bf16[1,10,2048]{2,1,0:T(8,128)(2,1)S(1)} %get-tuple-element.36), channel_id=1, source_target_pairs={{0,7},{1,0},{2,1},{3,2},{4,3},{5,4},{6,5},{7,6},{8,15},{9,8},{10,9... | collective-permute-start | bytes 122888 | tf_op jit(solution)/shard_map/ppermute | solution.py:28
  199.2 2.9 %collective-permute-start.20 = (bf16[1,10,2048]{2,1,0:T(8,128)(2,1)S(1)}, bf16[1,10,2048]{2,1,0:T(8,128)(2,1)S(1)}, u32[]{:S(2)}, u32[]{:S(2)}) collective-permute-start(bf16[1,10,2048]{2,1,0:T(8,128)(2,1)S(1)} %get-tuple-element.39), channel_id=1, source_target_pairs={{0,4},{1,5},{2,6},{3,7},{4,0},{5,1},{6,2},{7,3},{8,12},{9,13},{10,... | collective-permute-start | bytes 122888 | tf_op jit(solution)/shard_map/ppermute | solution.py:28
  202.3 5.9 %collective-permute-done.18 = bf16[1,10,2048]{2,1,0:T(8,128)(2,1)S(1)} collective-permute-done((bf16[1,10,2048]{2,1,0:T(8,128)(2,1)S(1)}, bf16[1,10,2048]{2,1,0:T(8,128)(2,1)S(1)}, u32[]{:S(2)}, u32[]{:S(2)}) %collective-permute-start.18) | collective-permute-done | bytes 40992 | tf_op jit(solution)/shard_map/ppermute | solution.py:28
  208.5 6.5 %collective-permute-done.19 = bf16[1,10,2048]{2,1,0:T(8,128)(2,1)S(1)} collective-permute-done((bf16[1,10,2048]{2,1,0:T(8,128)(2,1)S(1)}, bf16[1,10,2048]{2,1,0:T(8,128)(2,1)S(1)}, u32[]{:S(2)}, u32[]{:S(2)}) %collective-permute-start.19) | collective-permute-done | bytes 40992 | tf_op jit(solution)/shard_map/ppermute | solution.py:28
  216.1 8.4 %all_to_all.34 = bf16[8,8,2048]{2,1,0:T(8,128)(2,1)S(1)} all-to-all(bf16[8,8,2048]{2,1,0:T(8,128)(2,1)S(1)} %fusion.17), channel_id=1, replica_groups=mesh['roll'=4,'tp'=8] {'roll'}, dimensions={0} | all-to-all | bytes 524288 | tf_op jit(solution)/shard_map/all_to_all | solution.py:144
  (196 shorter events, 59.1 us)
Async XLA Ops:
  3.2 14.7 %all-to-all-start = ((s32[4,1,12]{2,1,0:T(1,128)}), s32[4,1,12]{2,1,0:T(1,128)S(1)}, u32[]{:S(2)}, u32[]{:S(2)}) async-start(s32[4,1,12]{2,1,0:T(1,128)} %broadcast_in_dim.29), calls=%async_computation | async-start | bytes 4096 | tf_op jit(solution)/shard_map/all_to_all | solution.py:105
  11.2 12.1 %collective-permute-start.1 = (bf16[192,2048]{1,0:T(8,128)(2,1)}, bf16[192,2048]{1,0:T(8,128)(2,1)}, u32[]{:S(2)}, u32[]{:S(2)}) collective-permute-start(bf16[192,2048]{1,0:T(8,128)(2,1)} %select_bitcast_fusion.1), channel_id=1, source_target_pairs={{0,8},{8,0},{16,24},{24,16},{1,9},{9,1},{17,25},{25,17},{2,10},{10... | collective-permute-start | bytes 2359304 | tf_op jit(solution)/shard_map/ppermute | solution.py:59
  13.7 12.5 %collective-permute-start = (bf16[1024,768]{1,0:T(8,128)(2,1)}, bf16[1024,768]{1,0:T(8,128)(2,1)}, u32[]{:S(2)}, u32[]{:S(2)}) collective-permute-start(bf16[1024,768]{1,0:T(8,128)(2,1)} %select_bitcast_fusion), channel_id=1, source_target_pairs={{0,8},{8,0},{16,24},{24,16},{1,9},{9,1},{17,25},{25,17},{2,10},{10... | collective-permute-start | bytes 4718600 | tf_op jit(solution)/shard_map/ppermute | solution.py:59
  19.9 9.8 %all-to-all-start.1 = ((bf16[8,8,2048]{2,1,0:T(8,128)(2,1)}), bf16[8,8,2048]{2,1,0:T(8,128)(2,1)S(1)}, u32[]{:S(2)}, u32[]{:S(2)}) async-start(bf16[8,8,2048]{2,1,0:T(8,128)(2,1)} %copy.15), calls=%async_computation.1 | async-start | bytes 524288 | tf_op jit(solution)/shard_map/all_to_all | solution.py:192
  29.6 54.7 %collective-permute-start.2 = (bf16[1024,768]{1,0:T(8,128)(2,1)}, bf16[1024,768]{1,0:T(8,128)(2,1)}, u32[]{:S(2)}, u32[]{:S(2)}) collective-permute-start(bf16[1024,768]{1,0:T(8,128)(2,1)} %get-tuple-element.12), channel_id=1, source_target_pairs={{0,16},{8,24},{16,0},{24,8},{1,17},{9,25},{17,1},{25,9},{2,18},{10... | collective-permute-start | bytes 4718600 | tf_op jit(solution)/shard_map/ppermute | solution.py:59
  32.0 51.5 %collective-permute-start.3 = (bf16[192,2048]{1,0:T(8,128)(2,1)}, bf16[192,2048]{1,0:T(8,128)(2,1)S(1)}, u32[]{:S(2)}, u32[]{:S(2)}) collective-permute-start(bf16[192,2048]{1,0:T(8,128)(2,1)} %get-tuple-element.13), channel_id=1, source_target_pairs={{0,16},{8,24},{16,0},{24,8},{1,17},{9,25},{17,1},{25,9},{2,18},{10... | collective-permute-start | bytes 2359304 | tf_op jit(solution)/shard_map/ppermute | solution.py:59
  33.3 20.9 %all-to-all-start.2 = ((bf16[8,10,2048]{2,1,0:T(8,128)(2,1)}), bf16[8,10,2048]{2,1,0:T(8,128)(2,1)}, u32[]{:S(2)}, u32[]{:S(2)}) async-start(bf16[8,10,2048]{2,1,0:T(8,128)(2,1)} %reshape.275), calls=%async_computation.2 | async-start | bytes 1048576 | tf_op jit(solution)/shard_map/all_to_all | solution.py:164
  86.2 9.2 %collective-permute-start.4 = (bf16[1024,768]{1,0:T(8,128)(2,1)S(1)}, bf16[1024,768]{1,0:T(8,128)(2,1)}, u32[]{:S(2)}, u32[]{:S(2)}) collective-permute-start(bf16[1024,768]{1,0:T(8,128)(2,1)S(1)} %add.223), channel_id=1, source_target_pairs={{0,8},{8,0},{16,24},{24,16},{1,9},{9,1},{17,25},{25,17},{2,10},{10... | collective-permute-start | bytes 4718600 | tf_op jit(solution)/shard_map/ppermute | solution.py:59
  92.2 37.4 %collective-permute-start.13 = (bf16[1024,768]{1,0:T(8,128)(2,1)S(1)}, bf16[1024,768]{1,0:T(8,128)(2,1)}, u32[]{:S(2)}, u32[]{:S(2)}) collective-permute-start(bf16[1024,768]{1,0:T(8,128)(2,1)S(1)} %copy-done.2), channel_id=1, source_target_pairs={{0,16},{8,24},{16,0},{24,8},{1,17},{9,25},{17,1},{25,9},{2,18},{10... | collective-permute-start | bytes 4718600 | tf_op jit(solution)/shard_map/ppermute | solution.py:59
  99.0 36.4 %collective-permute-start.6 = (bf16[1,10,2048]{2,1,0:T(8,128)(2,1)}, bf16[1,10,2048]{2,1,0:T(8,128)(2,1)}, u32[]{:S(2)}, u32[]{:S(2)}) collective-permute-start(bf16[1,10,2048]{2,1,0:T(8,128)(2,1)} %get-tuple-element.50), channel_id=1, source_target_pairs={{0,1},{1,2},{2,3},{3,4},{4,5},{5,6},{6,7},{7,0},{8,9},{9,10},{10,1... | collective-permute-start | bytes 122888 | tf_op jit(solution)/shard_map/ppermute | solution.py:28
  102.7 58.1 %collective-permute-start.15 = (bf16[192,2048]{1,0:T(8,128)(2,1)}, bf16[192,2048]{1,0:T(8,128)(2,1)}, u32[]{:S(2)}, u32[]{:S(2)}) collective-permute-start(bf16[192,2048]{1,0:T(8,128)(2,1)} %get-tuple-element.18), channel_id=1, source_target_pairs={{0,16},{8,24},{16,0},{24,8},{1,17},{9,25},{17,1},{25,9},{2,18},{10... | collective-permute-start | bytes 2359304 | tf_op jit(solution)/shard_map/ppermute | solution.py:59
  103.1 49.9 %collective-permute-start.12 = (bf16[1,10,2048]{2,1,0:T(8,128)(2,1)S(1)}, bf16[1,10,2048]{2,1,0:T(8,128)(2,1)S(1)}, u32[]{:S(2)}, u32[]{:S(2)}) collective-permute-start(bf16[1,10,2048]{2,1,0:T(8,128)(2,1)S(1)} %get-tuple-element.44), channel_id=1, source_target_pairs={{0,7},{1,0},{2,1},{3,2},{4,3},{5,4},{6,5},{7,6},{8,15},{9,8},{10,9... | collective-permute-start | bytes 122888 | tf_op jit(solution)/shard_map/ppermute | solution.py:28
  106.2 46.9 %collective-permute-start.11 = (bf16[1,10,2048]{2,1,0:T(8,128)(2,1)S(1)}, bf16[1,10,2048]{2,1,0:T(8,128)(2,1)S(1)}, u32[]{:S(2)}, u32[]{:S(2)}) collective-permute-start(bf16[1,10,2048]{2,1,0:T(8,128)(2,1)S(1)} %get-tuple-element.45), channel_id=1, source_target_pairs={{0,6},{1,7},{2,0},{3,1},{4,2},{5,3},{6,4},{7,5},{8,14},{9,15},{10,... | collective-permute-start | bytes 122888 | tf_op jit(solution)/shard_map/ppermute | solution.py:28
  129.6 23.4 %collective-permute-start.10 = (bf16[1,10,2048]{2,1,0:T(8,128)(2,1)}, bf16[1,10,2048]{2,1,0:T(8,128)(2,1)S(1)}, u32[]{:S(2)}, u32[]{:S(2)}) collective-permute-start(bf16[1,10,2048]{2,1,0:T(8,128)(2,1)} %get-tuple-element.46), channel_id=1, source_target_pairs={{0,5},{1,6},{2,7},{3,0},{4,1},{5,2},{6,3},{7,4},{8,13},{9,14},{10,... | collective-permute-start | bytes 122888 | tf_op jit(solution)/shard_map/ppermute | solution.py:28
  153.0 37.7 %collective-permute-start.14 = (bf16[1024,768]{1,0:T(8,128)(2,1)S(1)}, bf16[1024,768]{1,0:T(8,128)(2,1)}, u32[]{:S(2)}, u32[]{:S(2)}) collective-permute-start(bf16[1024,768]{1,0:T(8,128)(2,1)S(1)} %add.253), channel_id=1, source_target_pairs={{0,8},{8,0},{16,24},{24,16},{1,9},{9,1},{17,25},{25,17},{2,10},{10... | collective-permute-start | bytes 4718600 | tf_op jit(solution)/shard_map/ppermute | solution.py:59
  157.3 9.4 %all-to-all-start.3 = ((bf16[4,2,8,2048]{3,2,1,0:T(8,128)(2,1)}), bf16[4,2,8,2048]{3,2,1,0:T(8,128)(2,1)S(1)}, u32[]{:S(2)}, u32[]{:S(2)}) async-start(bf16[4,2,8,2048]{3,2,1,0:T(8,128)(2,1)} %bitcast.138), calls=%async_computation.3 | async-start | bytes 524288 | tf_op jit(solution)/shard_map/all_to_all | solution.py:139
  162.4 12.6 %collective-permute-start.16 = (bf16[192,2048]{1,0:T(8,128)(2,1)S(1)}, bf16[192,2048]{1,0:T(8,128)(2,1)}, u32[]{:S(2)}, u32[]{:S(2)}) collective-permute-start(bf16[192,2048]{1,0:T(8,128)(2,1)S(1)} %add.255), channel_id=1, source_target_pairs={{0,8},{8,0},{16,24},{24,16},{1,9},{9,1},{17,25},{25,17},{2,10},{10... | collective-permute-start | bytes 2359304 | tf_op jit(solution)/shard_map/ppermute | solution.py:59
  170.9 18.7 %all-to-all-start.4 = ((bf16[8,10,2048]{2,1,0:T(8,128)(2,1)}), bf16[8,10,2048]{2,1,0:T(8,128)(2,1)}, u32[]{:S(2)}, u32[]{:S(2)}) async-start(bf16[8,10,2048]{2,1,0:T(8,128)(2,1)} %reshape.279), calls=%async_computation.4 | async-start | bytes 1048576 | tf_op jit(solution)/shard_map/all_to_all | solution.py:164
  194.4 7.7 %collective-permute-start.17 = (bf16[1,10,2048]{2,1,0:T(8,128)(2,1)S(1)}, bf16[1,10,2048]{2,1,0:T(8,128)(2,1)S(1)}, u32[]{:S(2)}, u32[]{:S(2)}) collective-permute-start(bf16[1,10,2048]{2,1,0:T(8,128)(2,1)S(1)} %get-tuple-element.42), channel_id=1, source_target_pairs={{0,1},{1,2},{2,3},{3,4},{4,5},{5,6},{6,7},{7,0},{8,9},{9,10},{10,1... | collective-permute-start | bytes 122888 | tf_op jit(solution)/shard_map/ppermute | solution.py:28
  195.9 19.2 %collective-permute-start.23 = (bf16[1,10,2048]{2,1,0:T(8,128)(2,1)S(1)}, bf16[1,10,2048]{2,1,0:T(8,128)(2,1)S(1)}, u32[]{:S(2)}, u32[]{:S(2)}) collective-permute-start(bf16[1,10,2048]{2,1,0:T(8,128)(2,1)S(1)} %get-tuple-element.36), channel_id=1, source_target_pairs={{0,7},{1,0},{2,1},{3,2},{4,3},{5,4},{6,5},{7,6},{8,15},{9,8},{10,9... | collective-permute-start | bytes 122888 | tf_op jit(solution)/shard_map/ppermute | solution.py:28
  199.2 15.9 %collective-permute-start.22 = (bf16[1,10,2048]{2,1,0:T(8,128)(2,1)S(1)}, bf16[1,10,2048]{2,1,0:T(8,128)(2,1)S(1)}, u32[]{:S(2)}, u32[]{:S(2)}) collective-permute-start(bf16[1,10,2048]{2,1,0:T(8,128)(2,1)S(1)} %get-tuple-element.37), channel_id=1, source_target_pairs={{0,6},{1,7},{2,0},{3,1},{4,2},{5,3},{6,4},{7,5},{8,14},{9,15},{10,... | collective-permute-start | bytes 122888 | tf_op jit(solution)/shard_map/ppermute | solution.py:28
  199.2 15.9 %collective-permute-start.21 = (bf16[1,10,2048]{2,1,0:T(8,128)(2,1)S(1)}, bf16[1,10,2048]{2,1,0:T(8,128)(2,1)S(1)}, u32[]{:S(2)}, u32[]{:S(2)}) collective-permute-start(bf16[1,10,2048]{2,1,0:T(8,128)(2,1)S(1)} %get-tuple-element.38), channel_id=1, source_target_pairs={{0,5},{1,6},{2,7},{3,0},{4,1},{5,2},{6,3},{7,4},{8,13},{9,14},{10,... | collective-permute-start | bytes 122888 | tf_op jit(solution)/shard_map/ppermute | solution.py:28
  199.2 15.9 %collective-permute-start.20 = (bf16[1,10,2048]{2,1,0:T(8,128)(2,1)S(1)}, bf16[1,10,2048]{2,1,0:T(8,128)(2,1)S(1)}, u32[]{:S(2)}, u32[]{:S(2)}) collective-permute-start(bf16[1,10,2048]{2,1,0:T(8,128)(2,1)S(1)} %get-tuple-element.39), channel_id=1, source_target_pairs={{0,4},{1,5},{2,6},{3,7},{4,0},{5,1},{6,2},{7,3},{8,12},{9,13},{10,... | collective-permute-start | bytes 122888 | tf_op jit(solution)/shard_map/ppermute | solution.py:28
  208.3 6.8 %collective-permute-start.19 = (bf16[1,10,2048]{2,1,0:T(8,128)(2,1)S(1)}, bf16[1,10,2048]{2,1,0:T(8,128)(2,1)S(1)}, u32[]{:S(2)}, u32[]{:S(2)}) collective-permute-start(bf16[1,10,2048]{2,1,0:T(8,128)(2,1)S(1)} %get-tuple-element.40), channel_id=1, source_target_pairs={{0,3},{1,4},{2,5},{3,6},{4,7},{5,0},{6,1},{7,2},{8,11},{9,12},{10,... | collective-permute-start | bytes 122888 | tf_op jit(solution)/shard_map/ppermute | solution.py:28
  (34 other events, 301.9 us)
